TPU v7x, 256 devices: a whole 4x4x8 slice. The times are simulated.
256 devices in a mesh: group: 8 (over y, core), rows: 32 (over z, x).
Axes of the slice: x: 4, y: 4, z: 8, core: 2. Of those that a mesh axis runs over, the one named last changes fastest.
Arguments:
- features: bfloat16 [131072, 8192], P(('group', 'rows')), may hold values from -6 to 6
- labels: int32 [131072], P(('group', 'rows')), may hold values from 0 to 15
- weights: float32 [16, 8192], replicated, may hold values from -0.0625 to 0.0625
Outputs:
- new_logits: float32 [16, 131072], P(None, ('group', 'rows'))
All inputs are finite; a program needn't handle non-finite values.
Results may differ from a plain program's by a relative error of at most 0.0048.
Values may be sent and summed in bfloat16 or wider, within the bound.
A program may use at most 64 MiB of HBM per device.

v0:
```python
import jax
import jax.numpy as jnp
from jax import lax
from jax.sharding import PartitionSpec as P

ITERS = 2


ridge = 0.001


def rows_product(left, data):
    return lax.dot_general(left, data, (((1,), (1,)), ((), ())), preferred_element_type=jnp.float32)


def per_device(features, labels, weights):
    local_rows = features.shape[0]
    group_count = lax.axis_size("group")
    shard_rows = local_rows * lax.axis_size("rows")
    total = shard_rows * group_count
    classes = weights.shape[0]
    logits = rows_product(weights.astype(jnp.bfloat16), features)
    prob = jax.nn.softmax(logits, axis=0)
    onehot = (labels[None, :] == jnp.arange(classes, dtype=jnp.int32)[:, None]).astype(jnp.float32)
    resid = (prob - onehot).astype(jnp.bfloat16)
    grad_term = jnp.dot(resid, features, preferred_element_type=jnp.float32)
    grad = lax.psum(grad_term, ("group", "rows")) / total + ridge * weights
    answer = jnp.zeros_like(grad)
    residual = -grad
    search = residual
    norm_now = jnp.sum(residual * residual)
    for step in range(ITERS):
        hessian_inner = rows_product(search.astype(jnp.bfloat16), features)
        term = jnp.dot(
            (prob * (hessian_inner - jnp.sum(prob * hessian_inner, axis=0, keepdims=True))).astype(
                jnp.bfloat16
            ),
            features,
            preferred_element_type=jnp.float32,
        )
        image = lax.psum(term, "rows") / shard_rows + ridge * search
        alpha = norm_now / jnp.sum(search * image)
        answer = answer + alpha * search
        residual = residual - alpha * image
        norm_next = jnp.sum(residual * residual)
        search = residual + norm_next / norm_now * search
        norm_now = norm_next
    step_mean = lax.psum(answer, "group") / group_count
    return logits + rows_product(step_mean.astype(jnp.bfloat16), features)


def solution(mesh):
    return jax.shard_map(
        per_device,
        mesh=mesh,
        in_specs=(P(("group", "rows"), None), P(("group", "rows")), P()),
        out_specs=P(None, ("group", "rows")),
        check_vma=False,
    )
```

profile of v0, /device:TPU:1, one launch (start us, length us, event | category | flops | bytes accessed | tf_op | source)
XLA Modules:
  0.0 669.8 jit_solution(4229598422583929173)
XLA Ops:
  6.5 0.0 copy-start.3
  6.5 0.0 all-reduce.5.cloned.1.call-start
  6.5 0.0 copy-start
  6.5 6.0 fusion.18
  12.5 0.0 copy-start.2
  12.6 0.0 copy-done.3
  12.6 0.0 copy-done
  12.6 2.0 fusion.8
  14.6 0.0 all-reduce.5.cloned.1.call-update
  14.6 0.0 all-reduce.7.cloned.1.call-start
  14.7 254.6 %all-reduce.5.cloned.1.call-done = f32[16,8192]{1,0:T(8,128)} async-done(((f32[16,8192]{1,0:T(8,128)}), f32[16,8192]{1,0:T(8,128)}) %all-reduce.5.cloned.1.call-update) | async-done | bytes 524304 | tf_op jit(solution)/shard_map/psum | solution.py:27
  269.2 0.0 copy-done.2
  269.2 1.1 multiply_add_fusion.3
  270.4 5.7 multiply_reduce_fusion.5
  276.0 5.4 fusion.9
  281.4 0.0 all-reduce.7.cloned.1.call-update
  281.5 0.0 all-reduce.9.cloned.1.call-start
  281.5 143.1 %all-reduce.7.cloned.1.call-done = f32[16,8192]{1,0:T(8,128)} async-done(((f32[16,8192]{1,0:T(8,128)}), f32[16,8192]{1,0:T(8,128)}) %all-reduce.7.cloned.1.call-update) | async-done | bytes 524304 | tf_op jit(solution)/shard_map/psum | solution.py:41
  424.6 1.9 multiply_reduce_fusion.2
  427.9 1.8 multiply_reduce_fusion.1
  431.0 5.9 multiply_reduce_fusion.4
  436.9 0.0 copy-start.1
  436.9 5.5 fusion.10
  442.4 0.0 all-reduce.9.cloned.1.call-update
  442.4 0.2 all-reduce.11.cloned.1.call-start
  442.6 144.3 %all-reduce.9.cloned.1.call-done = f32[16,8192]{1,0:T(8,128)} async-done(((f32[16,8192]{1,0:T(8,128)}), f32[16,8192]{1,0:T(8,128)}) %all-reduce.9.cloned.1.call-update) | async-done | bytes 524304 | tf_op jit(solution)/shard_map/psum | solution.py:41
  586.9 0.0 copy-done.1
  586.9 1.9 multiply_reduce_fusion
  590.3 1.0 multiply_add_fusion
  591.3 0.0 all-reduce.11.cloned.1.call-update
  591.3 65.5 %all-reduce.11.cloned.1.call-done = f32[16,8192]{1,0:T(8,128)} async-done(((f32[16,8192]{1,0:T(8,128)}), f32[16,8192]{1,0:T(8,128)}) %all-reduce.11.cloned.1.call-update) | async-done | bytes 524304 | tf_op jit(solution)/shard_map/psum | solution.py:48
  656.8 6.5 convolution_add_fusion
  (1 shorter events, 0.0 us)
Async XLA Ops:
  6.5 6.0 copy-start.3
  6.5 262.7 %all-reduce.5.cloned.1.call-start = ((), (), s32[]{:S(2)}) async-start(), calls=%async_computation | async-start | bytes 1048576 | tf_op jit(solution)/shard_map/psum | solution.py:27
  6.5 6.0 copy-start
  12.5 256.7 %copy-start.2 = (f32[16,8192]{1,0:T(8,128)S(1)}, f32[16,8192]{1,0:T(8,128)}, u32[]{:S(2)}) copy-start(f32[16,8192]{1,0:T(8,128)} %param.5) | copy-start | bytes 1572868
  14.6 410.0 %all-reduce.7.cloned.1.call-start = ((), (), s32[]{:S(2)}) async-start(), calls=%async_computation.1 | async-start | bytes 1048576 | tf_op jit(solution)/shard_map/psum | solution.py:41
  281.5 305.5 %all-reduce.9.cloned.1.call-start = ((), (), s32[]{:S(2)}) async-start(), calls=%async_computation.2 | async-start | bytes 1048576 | tf_op jit(solution)/shard_map/psum | solution.py:41
  436.9 150.0 %copy-start.1 = (f32[16,8192]{1,0:T(8,128)S(1)}, f32[16,8192]{1,0:T(8,128)}, u32[]{:S(2)}) copy-start(f32[16,8192]{1,0:T(8,128)} %all-reduce.7.cloned.1.call-done) | copy-start | bytes 1572868
  442.4 214.4 %all-reduce.11.cloned.1.call-start = ((), (), s32[]{:S(2)}) async-start(), calls=%async_computation.3 | async-start | bytes 1048576 | tf_op jit(solution)/shard_map/psum | solution.py:48
Sparse Core Ops, SparseCore 0:
  14.7 254.4 all-reduce.4
  281.6 142.9 all-reduce.6
  442.5 144.3 all-reduce.8
  591.4 65.3 all-reduce.10
where the time goes:
time: 671 us; the launch traced here: 670 us
  waiting for transfers between devices  608 us (91%)
  matrix products  36.9 us (5%)
  between operations  17.3 us (3%)
  other arithmetic  7.75 us (1%)
    psum x2, waiting for transfers between devices, per_device(): image = lax.psum(term, 'rows') / shard_rows + ridge * search  287 us
    psum x1, waiting for transfers between devices, per_device(): grad = lax.psum(grad_term, ('group', 'rows')) / total + ridge * weights  255 us
    psum x1, waiting for transfers between devices, per_device(): step_mean = lax.psum(answer, 'group') / group_count  65.5 us
    dot_general x4, matrix products, rows_product(): lax.dot_general(left, data, (((1,), (1,)), ((), ())), preferred_element_t...  24 us
  transfers between devices with their start and end apart: 4, of which 4 were waited for; matrix products, arithmetic and copies ran while one was open for 0% of the time, Pallas kernels for 0%

commit v1 on v0

v1 whole, which is shorter than its diff:
```python
import functools

import jax
import jax.numpy as jnp
from jax import lax
from jax.experimental import pallas as pl
from jax.experimental.pallas import tpu as pltpu
from jax.sharding import PartitionSpec as P

RIDGE = 0.001
MESH = pl.DeviceIdType.MESH
NT = (((1,), (1,)), ((), ()))
F32 = jnp.float32
BF16 = jnp.bfloat16


def rows_product(left, data):
    return lax.dot_general(left, data, NT, preferred_element_type=F32)


def total_of(array):
    return jnp.sum(jnp.sum(array, axis=0, keepdims=True), axis=1, keepdims=True)


def kernel(
    dims,
    labels_ref,
    w_hbm,
    f_hbm,
    out_ref,
    feat,
    wts,
    part,
    got,
    line_src,
    line,
    first,
    term,
    gotx,
    zsrc,
    gotz,
    sums,
    stat_src,
    stat_z,
    stat_y,
    load_sem,
    w_sem,
    send,
    recv,
    first_sem,
    agx_sem,
    bulk_sem,
    fwd_sem,
):
    ny, nz, nx = dims
    ng = 2 * ny
    classes, depth = wts.shape
    rows = feat.shape[0]
    slices = ng * nx
    wide = depth // slices
    block = depth // ng
    xblock = depth // nx
    zwide = xblock // nz
    shard_rows = rows * nz * nx
    total_rows = shard_rows * ng

    g, r = lax.axis_index("group"), lax.axis_index("rows")
    y, c = g // 2, g % 2
    z, x = r // nx, r % nx
    mine = g * nx + x

    def cols(start, size):
        return pl.ds(pl.multiple_of(start, 128), size)

    def push(src, dst, ssem, rsem, gg, zz, xx):
        pltpu.make_async_remote_copy(
            src_ref=src,
            dst_ref=dst,
            send_sem=ssem,
            recv_sem=rsem,
            device_id=(gg, zz * nx + xx),
            device_id_type=MESH,
        ).start()

    def wait(ref, sem):
        pltpu.make_async_copy(ref, ref, sem).wait()

    w_copy = pltpu.make_async_copy(w_hbm, wts, w_sem)
    w_copy.start()
    loads = []
    for k in range(ng):
        span = pl.ds(k * block, block)
        loads.append(pltpu.make_async_copy(f_hbm.at[:, span], feat.at[:, span], load_sem.at[k]))
        loads[-1].start()
    barrier = pltpu.get_barrier_semaphore()

    def greet(k, carry):
        j = (mine + k) % slices
        pl.semaphore_signal(barrier, 1, device_id=(j // nx, z * nx + j % nx), device_id_type=MESH)
        return carry

    lax.fori_loop(1, slices, greet, 0)
    for k in range(1, nz):
        pl.semaphore_signal(barrier, 1, device_id=(g, ((z + k) % nz) * nx + x), device_id_type=MESH)

    w_copy.wait()
    logits = jnp.zeros((classes, rows), F32)
    for k in range(ng):
        loads[k].wait()
        span = slice(k * block, (k + 1) * block)
        logits += rows_product(wts[:, span].astype(BF16), feat[:, span])
    e = jnp.exp(logits - jnp.max(logits, axis=0, keepdims=True))
    prob = e / jnp.sum(e, axis=0, keepdims=True)
    onehot = labels_ref[...] == lax.broadcasted_iota(jnp.int32, (classes, rows), 0)
    resid = (prob - onehot.astype(F32)).astype(BF16)

    pl.semaphore_wait(barrier, slices - 1 + nz - 1)
    for k in list(range(1, ng)) + [0]:
        gg = (g + k) % ng
        span = cols(gg * block, block)
        part[:, span] = jnp.dot(resid, feat[:, span], preferred_element_type=F32).astype(BF16)
        for i in range(nx):
            if k == 0 and i == 0:
                continue
            xx = (x + i) % nx
            push(part.at[:, cols(gg * block + xx * wide, wide)], got.at[mine], send.at[0], recv.at[0], gg, z, xx)
    got[mine] = part[:, cols(mine * wide, wide)]
    wait(got.at[pl.ds(0, slices - 1)], recv.at[0])
    share = jnp.zeros((classes, wide), F32)
    for k in range(slices):
        share += got[k].astype(F32)
    line_src[...] = share.astype(BF16)
    for k in range(1, nz):
        push(line_src, line.at[z], send.at[1], recv.at[1], g, (z + k) % nz, x)
    line[z] = line_src[...]
    wait(line.at[pl.ds(0, nz - 1)], recv.at[1])
    share = jnp.zeros((classes, wide), F32)
    for k in range(nz):
        share += line[k].astype(F32)
    own = cols(mine * wide, wide)
    first[:, own] = (-(share / total_rows + RIDGE * wts[:, own])).astype(BF16)

    def spread(k, carry):
        j = (mine + k) % slices
        push(first.at[:, own], first.at[:, own], send.at[2], first_sem.at[g], j // nx, z, j % nx)
        return carry

    lax.fori_loop(1, slices, spread, 0)

    u1 = jnp.zeros((classes, rows), F32)
    for k in range(ng):
        gg = (g + k) % ng
        span = cols(gg * block, block)
        if k == 0:
            wait(got.at[pl.ds(0, nx - 1)], first_sem.at[gg])
        else:
            wait(first.at[:, span], first_sem.at[gg])
        u1 += rows_product(first[:, span], feat[:, span])
    c1 = (prob * (u1 - jnp.sum(prob * u1, axis=0, keepdims=True))).astype(BF16)

    for k in list(range(1, nx)) + [0]:
        xx = (x + k) % nx
        span = cols(xx * xblock, xblock)
        term[:, span] = jnp.dot(c1, feat[:, span], preferred_element_type=F32).astype(BF16)
        if k:
            push(term.at[:, span], gotx.at[x], send.at[3], recv.at[3], g, z, xx)
    gotx[x] = term[:, cols(x * xblock, xblock)]
    rr0 = jnp.zeros((1, 1), F32)
    for k in range(ng):
        r0 = first[:, k * block : (k + 1) * block].astype(F32)
        rr0 += total_of(r0 * r0)
    wait(gotx.at[pl.ds(0, nx - 1)], recv.at[3])
    for k in range(nz):
        span = slice(k * zwide, (k + 1) * zwide)
        share = jnp.zeros((classes, zwide), F32)
        for i in range(nx):
            share += gotx[i, :, span].astype(F32)
        zsrc[k] = share.astype(BF16)
    for k in range(1, nz):
        zz = (z + k) % nz
        push(zsrc.at[zz], gotz.at[z], send.at[4], recv.at[4], g, zz, x)
    gotz[z] = zsrc[z]
    wait(gotz.at[pl.ds(0, nz - 1)], recv.at[4])
    share = jnp.zeros((classes, zwide), F32)
    for k in range(nz):
        share += gotz[k].astype(F32)

    slot = c * ny + y
    own = cols(x * xblock + z * zwide, zwide)
    sums[slot, :, own] = share.astype(BF16)
    for k in range(1, nz):
        push(sums.at[slot, :, own], sums.at[slot, :, own], send.at[5], recv.at[5], g, (z + k) % nz, x)
    wait(gotz.at[pl.ds(0, nz - 1)], recv.at[5])

    def on_to_others(span):
        for k in range(1, ny):
            yy = (y + k) % ny
            push(sums.at[slot, :, span], sums.at[slot, :, span], send.at[7], bulk_sem.at[y], yy * 2 + c, z, x)
        push(sums.at[slot, :, span], sums.at[slot, :, span], send.at[8], fwd_sem.at[y], y * 2 + 1 - c, z, x)

    own = cols(x * xblock, xblock)
    for k in range(1, nx):
        push(sums.at[slot, :, own], sums.at[slot, :, own], send.at[6], agx_sem.at[x], g, z, (x + k) % nx)
    on_to_others(own)
    w1 = rows_product(sums[slot, :, own], feat[:, own])
    for k in (1, nx - 1, *range(2, nx - 1)) if nx > 2 else (1,):
        xx = (x + k) % nx
        span = cols(xx * xblock, xblock)
        wait(sums.at[slot, :, span], agx_sem.at[xx])
        on_to_others(span)
        w1 += rows_product(sums[slot, :, span], feat[:, span])

    r0_hp = jnp.zeros((1, 1), F32)
    for k in range(ng):
        span = slice(k * block, (k + 1) * block)
        r0 = first[:, span].astype(F32)
        hp = sums[slot, :, span].astype(F32) / shard_rows + RIDGE * r0
        r0_hp += total_of(r0 * hp)
    alpha1 = rr0 / r0_hp
    rr1 = jnp.zeros((1, 1), F32)
    for k in range(ng):
        span = slice(k * block, (k + 1) * block)
        r0 = first[:, span].astype(F32)
        hp = sums[slot, :, span].astype(F32) / shard_rows + RIDGE * r0
        r1 = r0 - alpha1 * hp
        rr1 += total_of(r1 * r1)
    beta = rr1 / rr0
    pp = jnp.zeros((1, 1), F32)
    for k in range(ng):
        span = slice(k * block, (k + 1) * block)
        r0 = first[:, span].astype(F32)
        hp = sums[slot, :, span].astype(F32) / shard_rows + RIDGE * r0
        p2 = r0 - alpha1 * hp + beta * r0
        pp += total_of(p2 * p2)
    u2 = u1 + beta * u1 - alpha1 * (w1 / shard_rows + RIDGE * u1)
    c2 = (prob * (u2 - jnp.sum(prob * u2, axis=0, keepdims=True))).astype(BF16).astype(F32)
    curve = total_of(c2 * u2)

    row = lax.broadcasted_iota(jnp.int32, (8, 128), 0)
    rest = jnp.where(row == 1, rr1, jnp.where(row == 2, pp, jnp.where(row == 3, alpha1, beta)))
    stat_src[0] = jnp.where(row == 0, curve, rest)
    for k in range(1, nz):
        push(stat_src.at[0], stat_z.at[z], send.at[9], recv.at[6], g, (z + k) % nz, x)
    stat_z[z] = stat_src[0]
    wait(stat_z.at[pl.ds(0, nz - 1)], recv.at[6])
    curve = jnp.zeros((8, 128), F32)
    for k in range(nz):
        curve += stat_z[k]
    stat_src[1] = jnp.where(row == 0, curve, rest)

    def tell(k, carry):
        j = (mine + k) % slices
        push(stat_src.at[1], stat_y.at[mine], send.at[10], recv.at[7], j // nx, z, j % nx)
        return carry

    lax.fori_loop(1, slices, tell, 0)
    stat_y[mine] = stat_src[1]

    for k in range(1, ny):
        yy = (y + k) % ny
        there = sums.at[c * ny + yy]
        wait(there, bulk_sem.at[yy])
        push(there, there, send.at[11], fwd_sem.at[yy], y * 2 + 1 - c, z, x)
    for k in range(ny):
        wait(sums.at[(1 - c) * ny + k], fwd_sem.at[k])
    w_all = jnp.zeros((ng * classes, rows), F32)
    for k in range(ng):
        span = slice(k * block, (k + 1) * block)
        w_all += rows_product(sums[:, :, span].reshape(ng * classes, block), feat[:, span])

    wait(stat_y.at[pl.ds(0, slices - 1)], recv.at[7])
    scale = jnp.zeros((1, 1), F32)
    result = logits
    for core in range(2):
        for yy in range(ny):
            at = (yy * 2 + core) * nx
            stats = stat_y[at]
            for i in range(1, nx):
                stats = jnp.where(row == 0, stats + stat_y[at + i], stats)
            curve, rr, pp, alpha, beta = (stats[i : i + 1, 0:1] for i in range(5))
            alpha2 = rr / (curve / shard_rows + RIDGE * pp)
            scale += alpha + alpha2 * (1.0 + beta - RIDGE * alpha)
            there = (core * ny + yy) * classes
            result -= (alpha * alpha2 / (ng * shard_rows)) * w_all[there : there + classes]
    out_ref[...] = result + (scale / ng) * u1

    wait(got.at[pl.ds(0, slices - 1)], send.at[0])
    wait(line.at[pl.ds(0, nz - 1)], send.at[1])
    wait(got.at[pl.ds(0, slices - 1)], send.at[2])
    wait(gotx.at[pl.ds(0, nx - 1)], send.at[3])
    wait(gotz.at[pl.ds(0, nz - 1)], send.at[4])
    wait(gotz.at[pl.ds(0, nz - 1)], send.at[5])
    wait(gotx.at[pl.ds(0, nx - 1)], send.at[6])
    wait(sums.at[pl.ds(0, ny - 1)], send.at[7])
    wait(sums.at[0], send.at[8])
    wait(stat_z.at[pl.ds(0, nz - 1)], send.at[9])
    wait(stat_y.at[pl.ds(0, slices - 1)], send.at[10])
    wait(sums.at[pl.ds(0, ny - 1)], send.at[11])


def per_device(dims, features, labels, weights):
    ny, nz, nx = dims
    ng = 2 * ny
    rows, depth = features.shape
    classes = weights.shape[0]
    slices = ng * nx
    wide, xblock = depth // slices, depth // nx
    zwide = xblock // nz
    dma = pltpu.SemaphoreType.DMA
    return pl.pallas_call(
        functools.partial(kernel, dims),
        out_shape=jax.ShapeDtypeStruct((classes, rows), F32),
        in_specs=[
            pl.BlockSpec(memory_space=pltpu.VMEM),
            pl.BlockSpec(memory_space=pl.ANY),
            pl.BlockSpec(memory_space=pl.ANY),
        ],
        out_specs=pl.BlockSpec(memory_space=pltpu.VMEM),
        scratch_shapes=[
            pltpu.VMEM((rows, depth), BF16),
            pltpu.VMEM((classes, depth), F32),
            pltpu.VMEM((classes, depth), BF16),
            pltpu.VMEM((slices, classes, wide), BF16),
            pltpu.VMEM((classes, wide), BF16),
            pltpu.VMEM((nz, classes, wide), BF16),
            pltpu.VMEM((classes, depth), BF16),
            pltpu.VMEM((classes, depth), BF16),
            pltpu.VMEM((nx, classes, xblock), BF16),
            pltpu.VMEM((nz, classes, zwide), BF16),
            pltpu.VMEM((nz, classes, zwide), BF16),
            pltpu.VMEM((ng, classes, depth), BF16),
            pltpu.VMEM((2, 8, 128), F32),
            pltpu.VMEM((nz, 8, 128), F32),
            pltpu.VMEM((slices, 8, 128), F32),
            dma((ng,)),
            dma,
            dma((12,)),
            dma((8,)),
            dma((ng,)),
            dma((nx,)),
            dma((ny,)),
            dma((ny,)),
        ],
        compiler_params=pltpu.CompilerParams(
            vmem_limit_bytes=40 * 2**20, collective_id=0, has_side_effects=True
        ),
        name="newton_step",
    )(labels.reshape(1, rows), weights, features)


def solution(mesh, nx=4):
    dims = (mesh.shape["group"] // 2, mesh.shape["rows"] // nx, nx)
    return jax.shard_map(
        functools.partial(per_device, dims),
        mesh=mesh,
        in_specs=(P(("group", "rows"), None), P(("group", "rows")), P()),
        out_specs=P(None, ("group", "rows")),
        check_vma=False,
    )
```

time: 671 us -> 72.9 us (0.11)
  waiting for transfers between devices: 608 us -> 0 us
  Pallas kernels: 0 us -> 67 us
  matrix products: 36.9 us -> 0 us
  between operations: 17.3 us -> 0.01 us
  other arithmetic: 7.75 us -> 0 us
    psum x4 -> x0, waiting for transfers between devices: 607 us -> none  [the longest x2 287 us: per_device(): image = lax.psum(term, 'rows') / shard_rows + ridge * search]
    pallas_call x0 -> x1, Pallas kernels: none -> 67 us  [per_device(): pl.pallas_call(functools.partial(kernel, dims), out_shape=jax.ShapeDtypeS...]
    dot_general x7 -> x0, matrix products: 36.9 us -> none  [the longest x4 24 us: rows_product(): lax.dot_general(left, data, (((1,), (1,)), ((), ())), preferred_element_t...]
  transfers between devices with their start and end apart: 4 -> 0, of which waited for: 4 -> 0; matrix products, arithmetic and copies ran while one was open for 0% -> 0% of each run, Pallas kernels for 0% -> 0%
where the time goes in v1:
time: 72.9 us; the launch traced here: 72.7 us
  Pallas kernels  67 us (92%)
  local copies, waits for them, and re-layouts  5.72 us (8%)
    pallas_call x1, Pallas kernels, per_device(): pl.pallas_call(functools.partial(kernel, dims), out_shape=jax.ShapeDtypeS...  67 us
    unnamed x7, local copies, waits for them, and re-layouts  5.72 us

profile of v1, /device:TPU:1, one launch (start us, length us, event | category | flops | bytes accessed | tf_op | source)
XLA Modules:
  0.0 72.7 jit_solution(143251013083046724)
XLA Ops:
  0.0 0.0 copy-start
  0.0 3.4 %copy-done = bf16[512,8192]{1,0:T(8,128)(2,1)S(1)} copy-done((bf16[512,8192]{1,0:T(8,128)(2,1)S(1)}, bf16[512,8192]{1,0:T(8,128)(2,1)}, u32[]{:S(2)}) %copy-start) | copy-done | bytes 8388632
  3.4 0.0 copy-start.1
  3.4 1.0 %copy-done.1 = f32[16,8192]{1,0:T(8,128)S(1)} copy-done((f32[16,8192]{1,0:T(8,128)S(1)}, f32[16,8192]{1,0:T(8,128)}, u32[]{:S(2)}) %copy-start.1) | copy-done | bytes 524312
  4.4 0.0 copy-start.2
  4.4 0.7 copy-done.2
  5.1 67.0 %newton_step.1 = f32[16,512]{1,0:T(8,128)S(1)} custom-call(s32[1,512]{1,0:T(1,128)S(1)} %bitcast.1, f32[16,8192]{1,0:T(8,128)S(1)} %copy-done.1, bf16[512,8192]{1,0:T(8,128)(2,1)S(1)} %copy-done), custom_call_target="tpu_custom_call" | custom-call | tf_op jit(solution)/shard_map/newton_step/pallas_call | solution.py:310
  72.1 0.6 copy.5
Async XLA Ops:
  0.0 3.4 %copy-start = (bf16[512,8192]{1,0:T(8,128)(2,1)S(1)}, bf16[512,8192]{1,0:T(8,128)(2,1)}, u32[]{:S(2)}) copy-start(bf16[512,8192]{1,0:T(8,128)(2,1)} %f_hbm.1) | copy-start | bytes 25165828
  3.4 1.0 %copy-start.1 = (f32[16,8192]{1,0:T(8,128)S(1)}, f32[16,8192]{1,0:T(8,128)}, u32[]{:S(2)}) copy-start(f32[16,8192]{1,0:T(8,128)} %w_hbm.1) | copy-start | bytes 1572868
  4.4 0.7 copy-start.2

commit v2 on v1

v2 whole, which is shorter than its diff:
```python
import functools

import jax
import jax.numpy as jnp
from jax import lax
from jax.experimental import pallas as pl
from jax.experimental.pallas import tpu as pltpu
from jax.sharding import PartitionSpec as P

RIDGE = 0.001
MESH = pl.DeviceIdType.MESH
NT = (((1,), (1,)), ((), ()))
F32 = jnp.float32
BF16 = jnp.bfloat16


def rows_product(left, data):
    return lax.dot_general(left, data, NT, preferred_element_type=F32)


def total_of(array):
    return jnp.sum(jnp.sum(array, axis=0, keepdims=True), axis=1, keepdims=True)


def near(n):
    return sorted(range(n), key=lambda k: min(k, n - k))


def kernel(
    dims,
    labels_hbm,
    w_hbm,
    f_hbm,
    out_ref,
    feat,
    labels,
    wts,
    pair_src,
    pair,
    part,
    got,
    line_src,
    line,
    first,
    term,
    gotx,
    zsrc,
    gotz,
    sums,
    stat_src,
    stat_z,
    stat_y,
    load_sem,
    w_sem,
    label_sem,
    send,
    recv,
    pair_sem,
    first_sem,
    cross_sem,
    rsx_sem,
    agz_sem,
    agx_sem,
    bulk_sem,
    fwd_sem,
):
    ny, nz, nx = dims
    ng = 2 * ny
    classes, depth = wts.shape
    rows = feat.shape[0]
    plane = ny * nx
    half = depth // 2
    block = half // ny
    wide = block // nx
    zblock = depth // nz
    zwide = zblock // nx
    shard_rows = rows * nz * nx
    total_rows = shard_rows * ng
    near_y, near_z, near_x = near(ny), near(nz), near(nx)

    g, r = lax.axis_index("group"), lax.axis_index("rows")
    y, c = g // 2, g % 2
    z, x = r // nx, r % nx
    slot = c * ny + y

    def cols(start, size):
        return pl.ds(pl.multiple_of(start, 128), size)

    def push(src, dst, ssem, rsem, yy, cc, zz, xx):
        pltpu.make_async_remote_copy(
            src_ref=src,
            dst_ref=dst,
            send_sem=ssem,
            recv_sem=rsem,
            device_id=(yy * 2 + cc, zz * nx + xx),
            device_id_type=MESH,
        ).start()

    def wait(ref, sem):
        pltpu.make_async_copy(ref, ref, sem).wait()

    w_copy = pltpu.make_async_copy(w_hbm, wts, w_sem)
    w_copy.start()
    label_copy = pltpu.make_async_copy(labels_hbm, labels, label_sem)
    label_copy.start()
    loads = []
    for k in range(ng):
        span = pl.ds(k * (depth // ng), depth // ng)
        loads.append(pltpu.make_async_copy(f_hbm.at[:, span], feat.at[:, span], load_sem.at[k]))
        loads[-1].start()
    barrier = pltpu.get_barrier_semaphore()
    others = [(j, k, i) for j in near_y[::-1] for k in near_x[::-1] for i in (1, 0) if (j, k, i) != (0, 0, 0)]
    others.sort(key=lambda o: -min(o[0], ny - o[0]) - min(o[1], nx - o[1]))
    for j, k, i in others:
        there = (((y + j) % ny) * 2 + (c + i) % 2, z * nx + (x + k) % nx)
        pl.semaphore_signal(barrier, 1, device_id=there, device_id_type=MESH)
    for k in near_z[:0:-1]:
        pl.semaphore_signal(barrier, 1, device_id=(g, ((z + k) % nz) * nx + x), device_id_type=MESH)

    w_copy.wait()
    logits = jnp.zeros((classes, rows), F32)
    for k in range(ng):
        loads[k].wait()
        span = slice(k * (depth // ng), (k + 1) * (depth // ng))
        logits += rows_product(wts[:, span].astype(BF16), feat[:, span])
    e = jnp.exp(logits - jnp.max(logits, axis=0, keepdims=True))
    prob = e / jnp.sum(e, axis=0, keepdims=True)
    label_copy.wait()
    onehot = labels[...] == lax.broadcasted_iota(jnp.int32, (classes, rows), 0)
    resid = (prob - onehot.astype(F32)).astype(BF16)

    pl.semaphore_wait(barrier, len(others) + nz - 1)
    for j in near_y[::-1]:
        yy = (y + j) % ny
        span = cols((1 - c) * half + yy * block, block)
        pair_src[yy] = jnp.dot(resid, feat[:, span], preferred_element_type=F32)
        push(pair_src.at[yy], pair.at[yy], send.at[0], pair_sem.at[yy], y, 1 - c, z, x)
    for j in near_y[::-1]:
        yy = (y + j) % ny
        begin = c * half + yy * block
        mine = jnp.dot(resid, feat[:, cols(begin, block)], preferred_element_type=F32)
        wait(pair.at[yy], pair_sem.at[yy])
        part[:, cols(begin, block)] = (mine + pair[yy]).astype(BF16)
        for k in near_x[::-1]:
            xx = (x + k) % nx
            if j or k:
                there = part.at[:, cols(begin + xx * wide, wide)]
                push(there, got.at[y * nx + x], send.at[1], recv.at[0], yy, c, z, xx)
    own = cols(slot * block + x * wide, wide)
    got[y * nx + x] = part[:, own]
    wait(got.at[pl.ds(0, plane - 1)], recv.at[0])
    share = jnp.zeros((classes, wide), F32)
    for k in range(plane):
        share += got[k].astype(F32)
    line_src[...] = share
    for k in near_z[:0:-1]:
        push(line_src, line.at[z], send.at[2], recv.at[1], y, c, (z + k) % nz, x)
    line[z] = line_src[...]
    wait(line.at[pl.ds(0, nz - 1)], recv.at[1])
    share = jnp.zeros((classes, wide), F32)
    for k in range(nz):
        share += line[k]
    first[:, own] = (-(share / total_rows + RIDGE * wts[:, own])).astype(BF16)
    for j, k, i in others:
        if i == 0:
            push(first.at[:, own], first.at[:, own], send.at[3], first_sem.at[y], (y + j) % ny, c, z, (x + k) % nx)

    u1 = jnp.zeros((classes, rows), F32)
    for j in near_y:
        yy = (y + j) % ny
        span = cols(c * half + yy * block, block)
        wait(got.at[pl.ds(0, nx if j else nx - 1)], first_sem.at[yy])
        push(first.at[:, span], first.at[:, span], send.at[4], cross_sem.at[yy], y, 1 - c, z, x)
        u1 += rows_product(first[:, span], feat[:, span])
    for j in near_y:
        yy = (y + j) % ny
        span = cols((1 - c) * half + yy * block, block)
        wait(first.at[:, span], cross_sem.at[yy])
        u1 += rows_product(first[:, span], feat[:, span])
    c1 = (prob * (u1 - jnp.sum(prob * u1, axis=0, keepdims=True))).astype(BF16)

    for k in near_z[::-1]:
        zz = (z + k) % nz
        begin = zz * zblock
        term[:, cols(begin, zblock)] = jnp.dot(
            c1, feat[:, cols(begin, zblock)], preferred_element_type=F32
        ).astype(BF16)
        for i in near_x[:0:-1]:
            xx = (x + i) % nx
            push(term.at[:, cols(begin + xx * zwide, zwide)], gotx.at[zz, x], send.at[5], rsx_sem.at[zz], y, c, z, xx)
        gotx[zz, x] = term[:, cols(begin + x * zwide, zwide)]
    rr0 = jnp.zeros((1, 1), F32)
    for k in range(ng):
        r0 = first[:, k * block : (k + 1) * block].astype(F32)
        rr0 += total_of(r0 * r0)
    for k in near_z[::-1]:
        zz = (z + k) % nz
        wait(gotx.at[zz, pl.ds(0, nx - 1)], rsx_sem.at[zz])
        share = jnp.zeros((classes, zwide), F32)
        for i in range(nx):
            share += gotx[zz, i].astype(F32)
        if k:
            zsrc[zz] = share.astype(BF16)
            push(zsrc.at[zz], gotz.at[z], send.at[6], recv.at[2], y, c, zz, x)
        else:
            gotz[z] = share.astype(BF16)
    wait(gotz.at[pl.ds(0, nz - 1)], recv.at[2])
    share = jnp.zeros((classes, zwide), F32)
    for k in range(nz):
        share += gotz[k].astype(F32)

    own = cols(z * zblock + x * zwide, zwide)
    sums[slot, :, own] = share.astype(BF16)
    for k in near_z[:0:-1]:
        push(sums.at[slot, :, own], sums.at[slot, :, own], send.at[7], agz_sem.at[z], y, c, (z + k) % nz, x)
    for k in near_z:
        zz = (z + k) % nz
        span = cols(zz * zblock + x * zwide, zwide)
        if k:
            wait(sums.at[slot, :, span], agz_sem.at[zz])
        for i in near_x[:0:-1]:
            push(sums.at[slot, :, span], sums.at[slot, :, span], send.at[8], agx_sem.at[zz], y, c, z, (x + i) % nx)

    w1 = jnp.zeros((classes, rows), F32)
    for n, k in enumerate(near_z):
        zz = (z + k) % nz
        span = cols(zz * zblock, zblock)
        wait(gotx.at[0, pl.ds(0, nx - 1)], agx_sem.at[zz])
        for j in near_y[:0:-1]:
            there = sums.at[slot, :, span]
            push(there, there, send.at[9], bulk_sem.at[y, n // (nz // 2)], (y + j) % ny, c, z, x)
        w1 += rows_product(sums[slot, :, span], feat[:, span])

    r0_hp = jnp.zeros((1, 1), F32)
    for k in range(ng):
        span = slice(k * block, (k + 1) * block)
        r0 = first[:, span].astype(F32)
        hp = sums[slot, :, span].astype(F32) / shard_rows + RIDGE * r0
        r0_hp += total_of(r0 * hp)
    alpha1 = rr0 / r0_hp
    rr1 = jnp.zeros((1, 1), F32)
    for k in range(ng):
        span = slice(k * block, (k + 1) * block)
        r0 = first[:, span].astype(F32)
        hp = sums[slot, :, span].astype(F32) / shard_rows + RIDGE * r0
        r1 = r0 - alpha1 * hp
        rr1 += total_of(r1 * r1)
    beta = rr1 / rr0
    pp = jnp.zeros((1, 1), F32)
    for k in range(ng):
        span = slice(k * block, (k + 1) * block)
        r0 = first[:, span].astype(F32)
        hp = sums[slot, :, span].astype(F32) / shard_rows + RIDGE * r0
        p2 = r0 - alpha1 * hp + beta * r0
        pp += total_of(p2 * p2)
    u2 = u1 + beta * u1 - alpha1 * (w1 / shard_rows + RIDGE * u1)
    c2 = (prob * (u2 - jnp.sum(prob * u2, axis=0, keepdims=True))).astype(BF16).astype(F32)
    curve = total_of(c2 * u2)

    row = lax.broadcasted_iota(jnp.int32, (8, 128), 0)
    rest = jnp.where(row == 1, rr1, jnp.where(row == 2, pp, jnp.where(row == 3, alpha1, beta)))
    stat_src[0] = jnp.where(row == 0, curve, rest)
    for k in near_z[:0:-1]:
        push(stat_src.at[0], stat_z.at[z], send.at[10], recv.at[3], y, c, (z + k) % nz, x)
    stat_z[z] = stat_src[0]
    push(sums.at[slot], sums.at[slot], send.at[11], recv.at[4], y, 1 - c, z, x)

    def pass_on(n):
        for j in near_y[1:]:
            yy = (y + j) % ny
            wait(sums.at[0, :, pl.ds(0, half)], bulk_sem.at[yy, n])
            for k in near_z[n * (nz // 2) : (n + 1) * (nz // 2)]:
                there = sums.at[c * ny + yy, :, cols(((z + k) % nz) * zblock, zblock)]
                push(there, there, send.at[12], fwd_sem.at[yy, n], y, 1 - c, z, x)

    def products(n):
        for j in near_y[1:]:
            wait(sums.at[0, :, pl.ds(0, half)], fwd_sem.at[(y + j) % ny, n])
        total = jnp.zeros((ng * classes, rows), F32)
        for k in near_z[n * (nz // 2) : (n + 1) * (nz // 2)]:
            span = cols(((z + k) % nz) * zblock, zblock)
            total += rows_product(sums[:, :, span].reshape(ng * classes, zblock), feat[:, span])
        return total

    pass_on(0)
    wait(stat_z.at[pl.ds(0, nz - 1)], recv.at[3])
    curve = jnp.zeros((8, 128), F32)
    for k in range(nz):
        curve += stat_z[k]
    stat_src[1] = jnp.where(row == 0, curve, rest)
    for j, k, i in others:
        push(
            stat_src.at[1], stat_y.at[slot * nx + x], send.at[13], recv.at[5],
            (y + j) % ny, (c + i) % 2, z, (x + k) % nx,
        )
    stat_y[slot * nx + x] = stat_src[1]
    wait(sums.at[0], recv.at[4])
    w_all = products(0)
    pass_on(1)
    w_all += products(1)

    wait(stat_y.at[pl.ds(0, ng * nx - 1)], recv.at[5])
    scale = jnp.zeros((1, 1), F32)
    result = logits
    for there in range(ng):
        stats = stat_y[there * nx]
        for i in range(1, nx):
            stats = jnp.where(row == 0, stats + stat_y[there * nx + i], stats)
        curve, rr, pp, alpha, beta = (stats[i : i + 1, 0:1] for i in range(5))
        alpha2 = rr / (curve / shard_rows + RIDGE * pp)
        scale += alpha + alpha2 * (1.0 + beta - RIDGE * alpha)
        result -= (alpha * alpha2 / (ng * shard_rows)) * w_all[there * classes : (there + 1) * classes]
    out_ref[...] = result + (scale / ng) * u1

    wait(pair_src, send.at[0])
    wait(got.at[pl.ds(0, plane - 1)], send.at[1])
    wait(line.at[pl.ds(0, nz - 1)], send.at[2])
    wait(got.at[pl.ds(0, plane - 1)], send.at[3])
    wait(first.at[:, pl.ds(0, half)], send.at[4])
    wait(gotx.at[:, pl.ds(0, nx - 1)], send.at[5])
    wait(gotz.at[pl.ds(0, nz - 1)], send.at[6])
    wait(gotz.at[pl.ds(0, nz - 1)], send.at[7])
    wait(gotx.at[:, pl.ds(0, nx - 1)], send.at[8])
    wait(sums.at[pl.ds(0, ny - 1)], send.at[9])
    wait(stat_z.at[pl.ds(0, nz - 1)], send.at[10])
    wait(sums.at[0], send.at[11])
    wait(sums.at[pl.ds(0, ny - 1)], send.at[12])
    wait(stat_y.at[pl.ds(0, ng * nx - 1)], send.at[13])


def per_device(dims, features, labels, weights):
    ny, nz, nx = dims
    ng = 2 * ny
    rows, depth = features.shape
    classes = weights.shape[0]
    block = depth // ng
    wide, zwide = block // nx, depth // (nz * nx)
    dma = pltpu.SemaphoreType.DMA
    any_space = pl.BlockSpec(memory_space=pl.ANY)
    return pl.pallas_call(
        functools.partial(kernel, dims),
        out_shape=jax.ShapeDtypeStruct((classes, rows), F32),
        in_specs=[any_space] * 3,
        out_specs=pl.BlockSpec(memory_space=pltpu.VMEM),
        scratch_shapes=[
            pltpu.VMEM((rows, depth), BF16),
            pltpu.VMEM((1, rows), jnp.int32),
            pltpu.VMEM((classes, depth), F32),
            pltpu.VMEM((ny, classes, block), F32),
            pltpu.VMEM((ny, classes, block), F32),
            pltpu.VMEM((classes, depth), BF16),
            pltpu.VMEM((ny * nx, classes, wide), BF16),
            pltpu.VMEM((classes, wide), F32),
            pltpu.VMEM((nz, classes, wide), F32),
            pltpu.VMEM((classes, depth), BF16),
            pltpu.VMEM((classes, depth), BF16),
            pltpu.VMEM((nz, nx, classes, zwide), BF16),
            pltpu.VMEM((nz, classes, zwide), BF16),
            pltpu.VMEM((nz, classes, zwide), BF16),
            pltpu.VMEM((ng, classes, depth), BF16),
            pltpu.VMEM((2, 8, 128), F32),
            pltpu.VMEM((nz, 8, 128), F32),
            pltpu.VMEM((ng * nx, 8, 128), F32),
            dma((ng,)),
            dma,
            dma,
            dma((14,)),
            dma((6,)),
            dma((ny,)),
            dma((ny,)),
            dma((ny,)),
            dma((nz,)),
            dma((nz,)),
            dma((nz,)),
            dma((ny, 2)),
            dma((ny, 2)),
        ],
        compiler_params=pltpu.CompilerParams(
            vmem_limit_bytes=60 * 2**20, collective_id=0, has_side_effects=True
        ),
        name="newton_step",
    )(labels.reshape(1, rows), weights, features)


def solution(mesh, nx=4):
    dims = (mesh.shape["group"] // 2, mesh.shape["rows"] // nx, nx)
    return jax.shard_map(
        functools.partial(per_device, dims),
        mesh=mesh,
        in_specs=(P(("group", "rows"), None), P(("group", "rows")), P()),
        out_specs=P(None, ("group", "rows")),
        check_vma=False,
    )
```

time: 72.9 us -> 63.6 us (0.87)
  Pallas kernels: 67 us -> 62.1 us
  local copies, waits for them, and re-layouts: 5.72 us -> 1.38 us
    pallas_call x1, Pallas kernels: 67 us -> 62.1 us  [per_device(): pl.pallas_call(functools.partial(kernel, dims), out_shape=jax.ShapeDtypeS...]
    unnamed x7 -> x1, local copies, waits for them, and re-layouts: 5.72 us -> 1.38 us
where the time goes in v2:
time: 63.6 us; the launch traced here: 63.5 us
  Pallas kernels  62.1 us (98%)
  local copies, waits for them, and re-layouts  1.38 us (2%)
    pallas_call x1, Pallas kernels, per_device(): pl.pallas_call(functools.partial(kernel, dims), out_shape=jax.ShapeDtypeS...  62.1 us
    unnamed x1, local copies, waits for them, and re-layouts  1.38 us

profile of v2, /device:TPU:1, one launch (start us, length us, event | category | flops | bytes accessed | tf_op | source)
XLA Modules:
  0.0 63.5 jit_solution(9180394648563227657)
XLA Ops:
  0.0 62.1 %newton_step.1 = f32[16,512]{1,0:T(8,128)} custom-call(s32[1,512]{1,0:T(1,128)} %bitcast.1, f32[16,8192]{1,0:T(8,128)} %w_hbm.1, bf16[512,8192]{1,0:T(8,128)(2,1)} %f_hbm.1), custom_call_target="tpu_custom_call" | custom-call | tf_op jit(solution)/shard_map/newton_step/pallas_call | solution.py:340
  62.1 1.4 %copy.5 = f32[16,512]{1,0:T(8,128)} copy(f32[16,512]{1,0:T(8,128)} %newton_step.1) | data formatting | bytes 65536

commit v3 on v2

--- a/solution.py
+++ b/solution.py
@@ -20,6 +20,12 @@
 
 def total_of(array):
     return jnp.sum(jnp.sum(array, axis=0, keepdims=True), axis=1, keepdims=True)
+
+
+def fold(array):
+    height, width = array.shape
+    array = sum(array[k : k + 8] for k in range(0, height, 8))
+    return sum(array[:, k : k + 128] for k in range(0, width, 128))
 
 
 def near(n):
@@ -33,6 +39,7 @@
     f_hbm,
     out_ref,
     feat,
+    feat_t,
     labels,
     wts,
     pair_src,
@@ -57,7 +64,6 @@
     recv,
     pair_sem,
     first_sem,
-    cross_sem,
     rsx_sem,
     agz_sem,
     agx_sem,
@@ -77,6 +83,7 @@
     shard_rows = rows * nz * nx
     total_rows = shard_rows * ng
     near_y, near_z, near_x = near(ny), near(nz), near(nx)
+    sides, across = near_y[1:3], near_y[3]
 
     g, r = lax.axis_index("group"), lax.axis_index("rows")
     y, c = g // 2, g % 2
@@ -116,6 +123,11 @@
         pl.semaphore_signal(barrier, 1, device_id=there, device_id_type=MESH)
     for k in near_z[:0:-1]:
         pl.semaphore_signal(barrier, 1, device_id=(g, ((z + k) % nz) * nx + x), device_id_type=MESH)
+
+    def turn(begin, end):
+        for k in range(begin, end):
+            span = slice(k * block, (k + 1) * block)
+            feat_t[span, :] = feat[:, span].T
 
     w_copy.wait()
     logits = jnp.zeros((classes, rows), F32)
@@ -148,6 +160,7 @@
                 push(there, got.at[y * nx + x], send.at[1], recv.at[0], yy, c, z, xx)
     own = cols(slot * block + x * wide, wide)
     got[y * nx + x] = part[:, own]
+    turn(0, ng // 2)
     wait(got.at[pl.ds(0, plane - 1)], recv.at[0])
     share = jnp.zeros((classes, wide), F32)
     for k in range(plane):
@@ -156,27 +169,23 @@
     for k in near_z[:0:-1]:
         push(line_src, line.at[z], send.at[2], recv.at[1], y, c, (z + k) % nz, x)
     line[z] = line_src[...]
+    turn(ng // 2, ng)
     wait(line.at[pl.ds(0, nz - 1)], recv.at[1])
     share = jnp.zeros((classes, wide), F32)
     for k in range(nz):
         share += line[k]
     first[:, own] = (-(share / total_rows + RIDGE * wts[:, own])).astype(BF16)
     for j, k, i in others:
-        if i == 0:
-            push(first.at[:, own], first.at[:, own], send.at[3], first_sem.at[y], (y + j) % ny, c, z, (x + k) % nx)
+        there = first.at[:, own]
+        push(there, there, send.at[3], first_sem.at[slot], (y + j) % ny, (c + i) % 2, z, (x + k) % nx)
 
     u1 = jnp.zeros((classes, rows), F32)
     for j in near_y:
-        yy = (y + j) % ny
-        span = cols(c * half + yy * block, block)
-        wait(got.at[pl.ds(0, nx if j else nx - 1)], first_sem.at[yy])
-        push(first.at[:, span], first.at[:, span], send.at[4], cross_sem.at[yy], y, 1 - c, z, x)
-        u1 += rows_product(first[:, span], feat[:, span])
-    for j in near_y:
-        yy = (y + j) % ny
-        span = cols((1 - c) * half + yy * block, block)
-        wait(first.at[:, span], cross_sem.at[yy])
-        u1 += rows_product(first[:, span], feat[:, span])
+        for i in (0, 1):
+            there = (c + i) % 2 * ny + (y + j) % ny
+            span = cols(there * block, block)
+            wait(got.at[pl.ds(0, nx if i or j else nx - 1)], first_sem.at[there])
+            u1 += jnp.dot(first[:, span], feat_t[span, :], preferred_element_type=F32)
     c1 = (prob * (u1 - jnp.sum(prob * u1, axis=0, keepdims=True))).astype(BF16)
 
     for k in near_z[::-1]:
@@ -189,10 +198,11 @@
             xx = (x + i) % nx
             push(term.at[:, cols(begin + xx * zwide, zwide)], gotx.at[zz, x], send.at[5], rsx_sem.at[zz], y, c, z, xx)
         gotx[zz, x] = term[:, cols(begin + x * zwide, zwide)]
-    rr0 = jnp.zeros((1, 1), F32)
+    r0_r0 = jnp.zeros((8, 128), F32)
     for k in range(ng):
         r0 = first[:, k * block : (k + 1) * block].astype(F32)
-        rr0 += total_of(r0 * r0)
+        r0_r0 += fold(r0 * r0)
+    rr0 = total_of(r0_r0)
     for k in near_z[::-1]:
         zz = (z + k) % nz
         wait(gotx.at[zz, pl.ds(0, nx - 1)], rsx_sem.at[zz])
@@ -211,17 +221,19 @@
 
     own = cols(z * zblock + x * zwide, zwide)
     sums[slot, :, own] = share.astype(BF16)
+    there = sums.at[slot, :, own]
     for k in near_z[:0:-1]:
-        push(sums.at[slot, :, own], sums.at[slot, :, own], send.at[7], agz_sem.at[z], y, c, (z + k) % nz, x)
+        push(there, there, send.at[7], agz_sem.at[z], y, c, (z + k) % nz, x)
     for k in near_z:
         zz = (z + k) % nz
-        span = cols(zz * zblock + x * zwide, zwide)
+        there = sums.at[slot, :, cols(zz * zblock + x * zwide, zwide)]
         if k:
-            wait(sums.at[slot, :, span], agz_sem.at[zz])
+            wait(there, agz_sem.at[zz])
         for i in near_x[:0:-1]:
-            push(sums.at[slot, :, span], sums.at[slot, :, span], send.at[8], agx_sem.at[zz], y, c, z, (x + i) % nx)
+            push(there, there, send.at[8], agx_sem.at[zz], y, c, z, (x + i) % nx)
 
     w1 = jnp.zeros((classes, rows), F32)
+    r0_s = jnp.zeros((8, 128), F32)
     for n, k in enumerate(near_z):
         zz = (z + k) % nz
         span = cols(zz * zblock, zblock)
@@ -229,41 +241,30 @@
         for j in near_y[:0:-1]:
             there = sums.at[slot, :, span]
             push(there, there, send.at[9], bulk_sem.at[y, n // (nz // 2)], (y + j) % ny, c, z, x)
-        w1 += rows_product(sums[slot, :, span], feat[:, span])
-
-    r0_hp = jnp.zeros((1, 1), F32)
-    for k in range(ng):
-        span = slice(k * block, (k + 1) * block)
-        r0 = first[:, span].astype(F32)
-        hp = sums[slot, :, span].astype(F32) / shard_rows + RIDGE * r0
-        r0_hp += total_of(r0 * hp)
-    alpha1 = rr0 / r0_hp
-    rr1 = jnp.zeros((1, 1), F32)
-    for k in range(ng):
-        span = slice(k * block, (k + 1) * block)
-        r0 = first[:, span].astype(F32)
-        hp = sums[slot, :, span].astype(F32) / shard_rows + RIDGE * r0
-        r1 = r0 - alpha1 * hp
-        rr1 += total_of(r1 * r1)
-    beta = rr1 / rr0
-    pp = jnp.zeros((1, 1), F32)
-    for k in range(ng):
-        span = slice(k * block, (k + 1) * block)
-        r0 = first[:, span].astype(F32)
-        hp = sums[slot, :, span].astype(F32) / shard_rows + RIDGE * r0
-        p2 = r0 - alpha1 * hp + beta * r0
-        pp += total_of(p2 * p2)
-    u2 = u1 + beta * u1 - alpha1 * (w1 / shard_rows + RIDGE * u1)
-    c2 = (prob * (u2 - jnp.sum(prob * u2, axis=0, keepdims=True))).astype(BF16).astype(F32)
-    curve = total_of(c2 * u2)
-
+        w1 += jnp.dot(sums[slot, :, span], feat_t[span, :], preferred_element_type=F32)
+        r0_s += fold(first[:, span].astype(F32) * sums[slot, :, span].astype(F32))
+
+    c_u1 = prob * (u1 - jnp.sum(prob * u1, axis=0, keepdims=True))
+    c_w1 = prob * (w1 - jnp.sum(prob * w1, axis=0, keepdims=True))
     row = lax.broadcasted_iota(jnp.int32, (8, 128), 0)
-    rest = jnp.where(row == 1, rr1, jnp.where(row == 2, pp, jnp.where(row == 3, alpha1, beta)))
-    stat_src[0] = jnp.where(row == 0, curve, rest)
+    three = [jnp.sum(fold(v), axis=0, keepdims=True) for v in (c_u1 * u1, c_u1 * w1, c_w1 * w1)]
+    stat_src[0] = jnp.where(row == 0, three[0], jnp.where(row == 1, three[1], three[2]))
     for k in near_z[:0:-1]:
         push(stat_src.at[0], stat_z.at[z], send.at[10], recv.at[3], y, c, (z + k) % nz, x)
     stat_z[z] = stat_src[0]
     push(sums.at[slot], sums.at[slot], send.at[11], recv.at[4], y, 1 - c, z, x)
+
+    alpha1 = rr0 / (total_of(r0_s) / shard_rows + RIDGE * rr0)
+    keep, drop = 1.0 - alpha1 * RIDGE, alpha1 / shard_rows
+    r1_r1 = jnp.zeros((8, 128), F32)
+    for k in range(ng):
+        span = slice(k * block, (k + 1) * block)
+        r1 = keep * first[:, span].astype(F32) - drop * sums[slot, :, span].astype(F32)
+        r1_r1 += fold(r1 * r1)
+    rr1 = total_of(r1_r1)
+    beta = rr1 / rr0
+    pp = rr1 + beta * beta * rr0
+    rest = jnp.where(row == 3, rr1, jnp.where(row == 4, pp, jnp.where(row == 5, alpha1, beta)))
 
     def pass_on(n):
         for j in near_y[1:]:
@@ -279,7 +280,8 @@
         total = jnp.zeros((ng * classes, rows), F32)
         for k in near_z[n * (nz // 2) : (n + 1) * (nz // 2)]:
             span = cols(((z + k) % nz) * zblock, zblock)
-            total += rows_product(sums[:, :, span].reshape(ng * classes, zblock), feat[:, span])
+            mine = sums[:, :, span].reshape(ng * classes, zblock)
+            total += jnp.dot(mine, feat_t[span, :], preferred_element_type=F32)
         return total
 
     pass_on(0)
@@ -287,7 +289,7 @@
     curve = jnp.zeros((8, 128), F32)
     for k in range(nz):
         curve += stat_z[k]
-    stat_src[1] = jnp.where(row == 0, curve, rest)
+    stat_src[1] = jnp.where(row < 3, curve, rest)
     for j, k, i in others:
         push(
             stat_src.at[1], stat_y.at[slot * nx + x], send.at[13], recv.at[5],
@@ -305,18 +307,20 @@
     for there in range(ng):
         stats = stat_y[there * nx]
         for i in range(1, nx):
-            stats = jnp.where(row == 0, stats + stat_y[there * nx + i], stats)
-        curve, rr, pp, alpha, beta = (stats[i : i + 1, 0:1] for i in range(5))
+            stats = jnp.where(row < 3, stats + stat_y[there * nx + i], stats)
+        uu, uw, ww = (jnp.sum(stats[i : i + 1], axis=1, keepdims=True) for i in range(3))
+        rr, pp, alpha, beta = (stats[i : i + 1, 0:1] for i in range(3, 7))
+        keep, drop = 1.0 + beta - RIDGE * alpha, alpha / shard_rows
+        curve = keep * keep * uu - 2.0 * keep * drop * uw + drop * drop * ww
         alpha2 = rr / (curve / shard_rows + RIDGE * pp)
-        scale += alpha + alpha2 * (1.0 + beta - RIDGE * alpha)
-        result -= (alpha * alpha2 / (ng * shard_rows)) * w_all[there * classes : (there + 1) * classes]
+        scale += alpha + alpha2 * keep
+        result -= (alpha2 * drop / ng) * w_all[there * classes : (there + 1) * classes]
     out_ref[...] = result + (scale / ng) * u1
 
     wait(pair_src, send.at[0])
     wait(got.at[pl.ds(0, plane - 1)], send.at[1])
     wait(line.at[pl.ds(0, nz - 1)], send.at[2])
-    wait(got.at[pl.ds(0, plane - 1)], send.at[3])
-    wait(first.at[:, pl.ds(0, half)], send.at[4])
+    wait(first.at[:, pl.ds(0, depth - wide)], send.at[3])
     wait(gotx.at[:, pl.ds(0, nx - 1)], send.at[5])
     wait(gotz.at[pl.ds(0, nz - 1)], send.at[6])
     wait(gotz.at[pl.ds(0, nz - 1)], send.at[7])
@@ -339,11 +343,12 @@
     any_space = pl.BlockSpec(memory_space=pl.ANY)
     return pl.pallas_call(
         functools.partial(kernel, dims),
-        out_shape=jax.ShapeDtypeStruct((classes, rows), F32),
+        out_shape=pltpu.VMEM((classes, rows), F32),
         in_specs=[any_space] * 3,
         out_specs=pl.BlockSpec(memory_space=pltpu.VMEM),
         scratch_shapes=[
             pltpu.VMEM((rows, depth), BF16),
+            pltpu.VMEM((depth, rows), BF16),
             pltpu.VMEM((1, rows), jnp.int32),
             pltpu.VMEM((classes, depth), F32),
             pltpu.VMEM((ny, classes, block), F32),
@@ -367,8 +372,7 @@
             dma((14,)),
             dma((6,)),
             dma((ny,)),
-            dma((ny,)),
-            dma((ny,)),
+            dma((ng,)),
             dma((nz,)),
             dma((nz,)),
             dma((nz,)),

time: 63.6 us -> 60.1 us (0.945)
  Pallas kernels: 62.1 us -> 59.5 us
  local copies, waits for them, and re-layouts: 1.38 us -> 0.62 us
    pallas_call x1, Pallas kernels: 62.1 us -> 59.5 us  [per_device(): pl.pallas_call(functools.partial(kernel, dims), out_shape=pltpu.VMEM((cla...]
    unnamed x1, local copies, waits for them, and re-layouts: 1.38 us -> 0.62 us
where the time goes in v3:
time: 60.1 us
  Pallas kernels  59.5 us (99%)
  local copies, waits for them, and re-layouts  0.62 us (1%)
    pallas_call x1, Pallas kernels, per_device(): pl.pallas_call(functools.partial(kernel, dims), out_shape=pltpu.VMEM((cla...  59.5 us

profile of v3, /device:TPU:1, one launch (start us, length us, event | category | flops | bytes accessed | tf_op | source)
XLA Modules:
  0.0 60.1 jit_solution(17529633145670794670)
XLA Ops:
  0.0 59.5 %newton_step.1 = f32[16,512]{1,0:T(8,128)S(1)} custom-call(s32[1,512]{1,0:T(1,128)} %bitcast.1, f32[16,8192]{1,0:T(8,128)} %w_hbm.1, bf16[512,8192]{1,0:T(8,128)(2,1)} %f_hbm.1), custom_call_target="tpu_custom_call" | custom-call | tf_op jit(solution)/shard_map/newton_step/pallas_call | solution.py:344
  59.5 0.6 %copy.5 = f32[16,512]{1,0:T(8,128)} copy(f32[16,512]{1,0:T(8,128)S(1)} %newton_step.1) | data formatting | bytes 65536

commit v4 on v3

--- a/solution.py
+++ b/solution.py
@@ -231,6 +231,7 @@
             wait(there, agz_sem.at[zz])
         for i in near_x[:0:-1]:
             push(there, there, send.at[8], agx_sem.at[zz], y, c, z, (x + i) % nx)
+        push(there, there, send.at[14], recv.at[6], (y + across) % ny, c, z, x)
 
     w1 = jnp.zeros((classes, rows), F32)
     r0_s = jnp.zeros((8, 128), F32)
@@ -238,7 +239,7 @@
         zz = (z + k) % nz
         span = cols(zz * zblock, zblock)
         wait(gotx.at[0, pl.ds(0, nx - 1)], agx_sem.at[zz])
-        for j in near_y[:0:-1]:
+        for j in sides:
             there = sums.at[slot, :, span]
             push(there, there, send.at[9], bulk_sem.at[y, n // (nz // 2)], (y + j) % ny, c, z, x)
         w1 += jnp.dot(sums[slot, :, span], feat_t[span, :], preferred_element_type=F32)
@@ -266,24 +267,44 @@
     pp = rr1 + beta * beta * rr0
     rest = jnp.where(row == 3, rr1, jnp.where(row == 4, pp, jnp.where(row == 5, alpha1, beta)))
 
+    def parts(n):
+        return [cols(((z + k) % nz) * zblock, zblock) for k in near_z[n * (nz // 2) : (n + 1) * (nz // 2)]]
+
+    def hand_over(yy, n):
+        for span in parts(n):
+            there = sums.at[c * ny + yy, :, span]
+            push(there, there, send.at[12], fwd_sem.at[yy, n], y, 1 - c, z, x)
+
     def pass_on(n):
-        for j in near_y[1:]:
+        for j in sides:
             yy = (y + j) % ny
             wait(sums.at[0, :, pl.ds(0, half)], bulk_sem.at[yy, n])
-            for k in near_z[n * (nz // 2) : (n + 1) * (nz // 2)]:
-                there = sums.at[c * ny + yy, :, cols(((z + k) % nz) * zblock, zblock)]
-                push(there, there, send.at[12], fwd_sem.at[yy, n], y, 1 - c, z, x)
+            hand_over(yy, n)
+
+    far_y = (y + across) % ny
+
+    def share_across():
+        wait(gotz, recv.at[6])
+        for zz in range(nz):
+            there = sums.at[c * ny + far_y, :, cols(zz * zblock + x * zwide, zwide)]
+            for i in near_x[:0:-1]:
+                push(there, there, send.at[4], recv.at[7], y, c, z, (x + i) % nx)
+
+    def finish_across():
+        wait(gotx.at[:, pl.ds(0, nx - 1)], recv.at[7])
+        hand_over(far_y, 0)
+        hand_over(far_y, 1)
 
     def products(n):
         for j in near_y[1:]:
             wait(sums.at[0, :, pl.ds(0, half)], fwd_sem.at[(y + j) % ny, n])
         total = jnp.zeros((ng * classes, rows), F32)
-        for k in near_z[n * (nz // 2) : (n + 1) * (nz // 2)]:
-            span = cols(((z + k) % nz) * zblock, zblock)
+        for span in parts(n):
             mine = sums[:, :, span].reshape(ng * classes, zblock)
             total += jnp.dot(mine, feat_t[span, :], preferred_element_type=F32)
         return total
 
+    share_across()
     pass_on(0)
     wait(stat_z.at[pl.ds(0, nz - 1)], recv.at[3])
     curve = jnp.zeros((8, 128), F32)
@@ -297,8 +318,9 @@
         )
     stat_y[slot * nx + x] = stat_src[1]
     wait(sums.at[0], recv.at[4])
+    finish_across()
+    pass_on(1)
     w_all = products(0)
-    pass_on(1)
     w_all += products(1)
 
     wait(stat_y.at[pl.ds(0, ng * nx - 1)], recv.at[5])
@@ -325,7 +347,9 @@
     wait(gotz.at[pl.ds(0, nz - 1)], send.at[6])
     wait(gotz.at[pl.ds(0, nz - 1)], send.at[7])
     wait(gotx.at[:, pl.ds(0, nx - 1)], send.at[8])
-    wait(sums.at[pl.ds(0, ny - 1)], send.at[9])
+    wait(gotx.at[:, pl.ds(0, nx - 1)], send.at[4])
+    wait(sums.at[pl.ds(0, 2)], send.at[9])
+    wait(gotz, send.at[14])
     wait(stat_z.at[pl.ds(0, nz - 1)], send.at[10])
     wait(sums.at[0], send.at[11])
     wait(sums.at[pl.ds(0, ny - 1)], send.at[12])
@@ -369,8 +393,8 @@
             dma((ng,)),
             dma,
             dma,
-            dma((14,)),
-            dma((6,)),
+            dma((15,)),
+            dma((8,)),
             dma((ny,)),
             dma((ng,)),
             dma((nz,)),

time: 60.1 us -> 58.6 us (0.975)
  Pallas kernels: 59.5 us -> 58 us
    pallas_call x1, Pallas kernels: 59.5 us -> 58 us  [per_device(): pl.pallas_call(functools.partial(kernel, dims), out_shape=pltpu.VMEM((cla...]
where the time goes in v4:
time: 58.6 us
  Pallas kernels  58 us (99%)
  local copies, waits for them, and re-layouts  0.62 us (1%)
    pallas_call x1, Pallas kernels, per_device(): pl.pallas_call(functools.partial(kernel, dims), out_shape=pltpu.VMEM((cla...  58 us

profile of v4, /device:TPU:1, one launch (start us, length us, event | category | flops | bytes accessed | tf_op | source)
XLA Modules:
  0.0 58.6 jit_solution(793222698370400836)
XLA Ops:
  0.0 58.0 %newton_step.1 = f32[16,512]{1,0:T(8,128)S(1)} custom-call(s32[1,512]{1,0:T(1,128)} %bitcast.1, f32[16,8192]{1,0:T(8,128)} %w_hbm.1, bf16[512,8192]{1,0:T(8,128)(2,1)} %f_hbm.1), custom_call_target="tpu_custom_call" | custom-call | tf_op jit(solution)/shard_map/newton_step/pallas_call | solution.py:368
  58.0 0.6 %copy.5 = f32[16,512]{1,0:T(8,128)} copy(f32[16,512]{1,0:T(8,128)S(1)} %newton_step.1) | data formatting | bytes 65536

commit v5 on v4

--- a/solution.py
+++ b/solution.py
@@ -111,8 +111,8 @@
     label_copy = pltpu.make_async_copy(labels_hbm, labels, label_sem)
     label_copy.start()
     loads = []
-    for k in range(ng):
-        span = pl.ds(k * (depth // ng), depth // ng)
+    for k in range(ng // 2):
+        span = pl.ds(k * 2 * block, 2 * block)
         loads.append(pltpu.make_async_copy(f_hbm.at[:, span], feat.at[:, span], load_sem.at[k]))
         loads[-1].start()
     barrier = pltpu.get_barrier_semaphore()
@@ -131,9 +131,9 @@
 
     w_copy.wait()
     logits = jnp.zeros((classes, rows), F32)
-    for k in range(ng):
+    for k in range(ng // 2):
         loads[k].wait()
-        span = slice(k * (depth // ng), (k + 1) * (depth // ng))
+        span = slice(k * 2 * block, (k + 1) * 2 * block)
         logits += rows_product(wts[:, span].astype(BF16), feat[:, span])
     e = jnp.exp(logits - jnp.max(logits, axis=0, keepdims=True))
     prob = e / jnp.sum(e, axis=0, keepdims=True)
@@ -390,7 +390,7 @@
             pltpu.VMEM((2, 8, 128), F32),
             pltpu.VMEM((nz, 8, 128), F32),
             pltpu.VMEM((ng * nx, 8, 128), F32),
-            dma((ng,)),
+            dma((ng // 2,)),
             dma,
             dma,
             dma((15,)),

time: 58.6 us -> 58.6 us (level)
  no operation moved by 1% of the time
where the time goes in v5:
time: 58.6 us; the launch traced here: 58.5 us
  Pallas kernels  57.9 us (99%)
  local copies, waits for them, and re-layouts  0.62 us (1%)
    pallas_call x1, Pallas kernels, per_device(): pl.pallas_call(functools.partial(kernel, dims), out_shape=pltpu.VMEM((cla...  57.9 us

profile of v5, /device:TPU:1, one launch (start us, length us, event | category | flops | bytes accessed | tf_op | source)
XLA Modules:
  0.0 58.5 jit_solution(9785727174183142360)
XLA Ops:
  0.0 57.9 %newton_step.1 = f32[16,512]{1,0:T(8,128)S(1)} custom-call(s32[1,512]{1,0:T(1,128)} %bitcast.1, f32[16,8192]{1,0:T(8,128)} %w_hbm.1, bf16[512,8192]{1,0:T(8,128)(2,1)} %f_hbm.1), custom_call_target="tpu_custom_call" | custom-call | tf_op jit(solution)/shard_map/newton_step/pallas_call | solution.py:368
  57.9 0.6 %copy.5 = f32[16,512]{1,0:T(8,128)} copy(f32[16,512]{1,0:T(8,128)S(1)} %newton_step.1) | data formatting | bytes 65536
